TPU v7x, 512 devices: a whole 4x4x16 slice. The times are simulated.
512 devices in a mesh: col: 16 (over z), row: 32 (over x, y, core).
Axes of the slice: x: 4, y: 4, z: 16, core: 2. Of those that a mesh axis runs over, the one named last changes fastest.
Arguments:
- out_grad: bfloat16 [131072, 256], P(('col', 'row')), may hold values from -6 to 6
- relu_mask: int32 [131072, 256], P(('col', 'row')), may hold values 0 or 1
- features: bfloat16 [131072, 256], P(('col', 'row')), may hold values from -0.0390625 to 0.0390625
- weight: bfloat16 [256, 256], replicated, may hold values from -0.375 to 0.375
- tile_values: bfloat16 [16, 32, 96, 128, 128], P('col', 'row'), may hold values from -0.125 to 0.125
- tile_index: int32 [16, 32, 96], P('col', 'row'), may hold values from 0 to 2047, as said below
- tile_count: int32 [16, 32], P('col', 'row'), may hold values from 1 to 96, as said below
Outputs:
- input_grad: bfloat16 [131072, 256], P(('col', 'row'))
- weight_grad: float32 [256, 256], replicated
Inputs may be any that keep to these rules, and one draw needn't show every extreme that they name: `tile_index`: within one device the 96 entries are distinct positions of its grid of 64 x 32 tiles. `tile_count`: at least 1; some device in every draw has all 96 slots live.
All inputs are finite; a program needn't handle non-finite values. No bound on the sum of `relu_mask` on one device may be relied on, other than what follows from the above.
Results may differ from a plain program's by a relative error of at most 0.0049.
Values may be sent and summed in bfloat16 or wider, within the bound.
A program may use at most 128 MiB of HBM per device.

v0:
```python
import jax
import jax.numpy as jnp
from jax import lax
from jax.sharding import PartitionSpec as P


def on_device(out_grad, relu_mask, features, weight, tile_values, tile_index, tile_count):
    gradient = (out_grad.astype(jnp.float32) * relu_mask.astype(jnp.float32)).astype(jnp.bfloat16)
    stripe = lax.all_gather(gradient, "row", axis=0, tiled=True)
    block_size = tile_values.shape[-1]
    width = gradient.shape[1]
    slot_count = tile_values.shape[2]
    col_count = lax.axis_size("col")
    segments = out_grad.shape[0] // block_size
    col_blocks = col_count * segments
    stripe_blocks = stripe.reshape(-1, block_size, width)
    index_list = tile_index.reshape(slot_count)
    tile_block = tile_values.reshape(slot_count, block_size, block_size)
    live_count = tile_count.reshape(())
    row_block = index_list // col_blocks
    col_block = index_list % col_blocks
    target = jnp.where(jnp.arange(slot_count) < live_count, col_block, col_blocks)
    products = jnp.einsum(
        "kab,kaf->kbf", tile_block, stripe_blocks[row_block], preferred_element_type=jnp.float32
    )
    partial_value = (
        jnp.zeros((col_blocks, block_size, width), jnp.float32)
        .at[target]
        .add(products, mode="drop")
    )
    partial_value = partial_value.reshape(col_count, segments * block_size, width)
    summed = lax.psum_scatter(partial_value, "col", scatter_dimension=0, tiled=True).reshape(
        segments * block_size, width
    )
    node_grad = summed.astype(jnp.bfloat16)
    input_grad = jnp.einsum(
        "no,io->ni", node_grad, weight, preferred_element_type=jnp.float32
    ).astype(jnp.bfloat16)
    local_weight = jnp.einsum("ni,no->io", features, node_grad, preferred_element_type=jnp.float32)
    weight_grad = lax.psum(local_weight, ("col", "row"))
    return (input_grad, weight_grad)


def solution(mesh):
    placed = (
        P(("col", "row"), None),
        P(("col", "row"), None),
        P(("col", "row"), None),
        P(),
        P("col", "row", None, None, None),
        P("col", "row", None),
        P("col", "row"),
    )
    return jax.shard_map(
        on_device,
        mesh=mesh,
        in_specs=placed,
        out_specs=(P(("col", "row"), None), P()),
        check_vma=False,
    )
```

profile of v0, /device:TPU:1, one launch (start us, length us, event | category | flops | bytes accessed | tf_op | source)
XLA Modules:
  0.0 685.8 jit_solution(6199799285801856658)
XLA Ops:
  7.2 0.0 copy-start
  7.2 0.0 all-gather.2.cloned.1.call-start
  7.2 1.8 multiply_convert_fusion
  9.0 0.0 all-gather.2.cloned.1.call-update
  9.1 0.0 reduce-scatter.2.cloned.1.call-start
  9.8 0.7 fusion.6
  10.5 68.4 %all-gather.2.cloned.1.call-done = bf16[8192,256]{1,0:T(8,128)(2,1)} async-done(((bf16[256,256]{1,0:T(8,128)(2,1)}), bf16[8192,256]{1,0:T(8,128)(2,1)}) %all-gather.2.cloned.1.call-update) | async-done | bytes 4194320 | tf_op jit(solution)/shard_map/all_gather | solution.py:9
  78.9 8.2 %gather_fusion = bf16[96,128,256]{2,1,0:T(8,128)(2,1)} fusion(bf16[64,128,256]{2,1,0:T(8,128)(2,1)} %bitcast.41, s32[1024]{0:T(1024)S(1)} %pad_clamp_fusion), kind=kCustom, calls=%fused_computation | custom fusion | bytes 12583296 | tf_op jit(solution)/shard_map/gather | solution.py:24
  87.0 0.0 copy-done
  87.0 9.1 %convolution_bitcast_fusion = f32[96,128,256]{1,2,0:T(8,128)} fusion(bf16[96,128,256]{2,1,0:T(8,128)(2,1)} %gather_fusion, bf16[1,1,96,128,128]{4,3,2,1,0:T(8,128)(2,1)S(1)} %copy-done), kind=kOutput, calls=%fused_computation.2 | convolution fusion | flops 805306368 | bytes 22020096 | tf_op jit(solution)/shard_map/kab,kaf->kbf/dot_general | solution.py:23
  96.1 12.6 %copy.12 = f32[96,128,256]{2,1,0:T(8,128)} copy(f32[96,128,256]{1,2,0:T(8,128)} %convolution_bitcast_fusion) | data formatting | bytes 25165824 | tf_op jit(solution)/shard_map/kab,kaf->kbf/dot_general | solution.py:23
  108.7 2.4 broadcast_in_dim.4
  111.1 0.0 copy-start.1
  111.1 28.3 %scatter_fusion = f32[32,128,256]{2,1,0:T(8,128)} fusion(f32[32,128,256]{2,1,0:T(8,128)} %broadcast_in_dim.4, s32[96]{0:T(128)S(1)} %get-tuple-element.7, f32[96,128,256]{2,1,0:T(8,128)} %copy.12), kind=kCustom, calls=%fused_computation.1 | custom fusion | flops 3145728 | bytes 37749120 | tf_op jit(solution)/shard_map/scatter-add | solution.py:29
  139.4 0.0 reduce-scatter.2.cloned.1.call-update
  139.4 0.0 all-reduce.2.cloned.1.call-start
  139.5 68.4 %reduce-scatter.2.cloned.1.call-done = f32[1,256,256]{2,1,0:T(8,128)} async-done(((f32[16,256,256]{2,1,0:T(8,128)}), f32[1,256,256]{2,1,0:T(8,128)}) %reduce-scatter.2.cloned.1.call-update) | async-done | bytes 262160 | tf_op jit(solution)/shard_map/reduce_scatter | solution.py:32
  207.9 0.0 copy-done.1
  207.9 1.9 convolution_bitcast_fusion.1
  209.8 0.0 all-reduce.2.cloned.1.call-update
  209.8 0.0 copy-done.2
  209.8 1.8 convolution_convert_fusion
  211.6 465.8 %all-reduce.2.cloned.1.call-done = f32[256,256]{0,1:T(8,128)} async-done(((f32[256,256]{0,1:T(8,128)}), f32[256,256]{0,1:T(8,128)}) %all-reduce.2.cloned.1.call-update) | async-done | bytes 262160 | tf_op jit(solution)/shard_map/psum | solution.py:40
  677.5 1.8 copy.13
  (2 shorter events, 0.0 us)
Async XLA Ops:
  7.2 79.9 %copy-start = (bf16[1,1,96,128,128]{4,3,2,1,0:T(8,128)(2,1)S(1)}, bf16[1,1,96,128,128]{4,3,2,1,0:T(8,128)(2,1)}, u32[]{:S(2)}) copy-start(bf16[1,1,96,128,128]{4,3,2,1,0:T(8,128)(2,1)} %param.11) | copy-start | bytes 9437188
  7.2 71.7 %all-gather.2.cloned.1.call-start = ((), (), s32[]{:S(2)}) async-start(), calls=%async_computation.1 | async-start | bytes 4325376 | tf_op jit(solution)/shard_map/all_gather | solution.py:9
  9.1 198.8 %reduce-scatter.2.cloned.1.call-start = ((), (), s32[]{:S(2)}) async-start(), calls=%async_computation.2 | async-start | bytes 4456448 | tf_op jit(solution)/shard_map/reduce_scatter | solution.py:32
  111.1 96.8 %copy-start.1 = (bf16[256,256]{1,0:T(8,128)(2,1)S(1)}, bf16[256,256]{1,0:T(8,128)(2,1)}, u32[]{:S(2)}) copy-start(bf16[256,256]{1,0:T(8,128)(2,1)} %param.9) | copy-start | bytes 393220
  111.1 98.7 %copy-start.2 = (bf16[256,256]{1,0:T(8,128)(2,1)S(1)}, bf16[256,256]{1,0:T(8,128)(2,1)}, u32[]{:S(2)}) copy-start(bf16[256,256]{1,0:T(8,128)(2,1)} %param.10) | copy-start | bytes 393220
  139.4 538.1 %all-reduce.2.cloned.1.call-start = ((), (), s32[]{:S(2)}) async-start(), calls=%async_computation.3 | async-start | bytes 524288 | tf_op jit(solution)/shard_map/psum | solution.py:40
Sparse Core Ops, SparseCore 0:
  11.7 67.0 all-gather.1
  139.5 68.3 reduce-scatter.1
  213.9 463.5 all-reduce.1
where the time goes:
time: 687 us; the launch traced here: 686 us
  waiting for transfers between devices  603 us (88%)
  other arithmetic  30.7 us (4%)
  local copies, waits for them, and re-layouts  25 us (4%)
  between operations  14.4 us (2%)
  matrix products  12.8 us (2%)
    psum x1, waiting for transfers between devices, on_device(): weight_grad = lax.psum(local_weight, ('col', 'row'))  466 us
    reduce_scatter x1, waiting for transfers between devices, on_device(): lax.psum_scatter(partial_value, 'col', scatter_dimension=0, tiled=True)  68.4 us
    all_gather x1, waiting for transfers between devices, on_device(): stripe = lax.all_gather(gradient, 'row', axis=0, tiled=True)  68.4 us
    scatter-add x1, other arithmetic, on_device(): partial_value = jnp.zeros((col_blocks, block_size, width), jnp.float32).a...  28.3 us
  transfers between devices with their start and end apart: 3, of which 3 were waited for; matrix products, arithmetic and copies ran while one was open for 0% of the time, Pallas kernels for 0%

commit v1 on v0

v1 whole, which is shorter than its diff:
```python
import jax
import jax.numpy as jnp
from jax import lax
from jax.experimental import pallas as pl
from jax.experimental.pallas import tpu as pltpu
from jax.sharding import PartitionSpec as P

MESH = pl.DeviceIdType.MESH
BLK = 128
F = 256
SLOTS = 96
N_COL = 16
N_ROW = 32
COLB = 32
STRIPE = 64
HALF = N_COL // 2
GROUP = 4
PIECES = 4
PIECE = F // PIECES
SIGN = (1, -1)


def farthest(e, way):
    return HALF if way == e % 2 else HALF - 1


def loop(begin, end, f):
    def one(i, _):
        f(i)
        return 0
    lax.fori_loop(begin, end, one, 0)


def kernel(
    count, index_hbm, grad_hbm, mask_hbm, feat_hbm, weight_hbm, tiles_hbm,
    input_out, weight_out,
    index_ref, meta_v, meta, grad_ref, mask_ref, feats, weight_ref, tiles, stripe_0, stripe_1, parts,
    sums_out, sums_in, node_t, total, dw, plane_in, line, done,
    load_sem, meta_sem, g_send, g_recv, f_send, f_recv, s_send, s_recv,
    a_send, a_recv, z_send, z_recv, b_send, b_recv,
):
    c = lax.axis_index("col")
    r = lax.axis_index("row")
    x, y, k = lax.div(r, 8), lax.rem(lax.div(r, 2), 4), lax.rem(r, 2)
    stripe = (stripe_0, stripe_1)

    def col(d):
        return lax.rem(c + d + N_COL, N_COL)

    def row(d):
        return lax.rem(r + d, N_ROW)

    def copy(src, dst, send, recv, device):
        return pltpu.make_async_remote_copy(
            src_ref=src, dst_ref=dst, send_sem=send, recv_sem=recv,
            device_id=device, device_id_type=MESH,
        )

    fetches = [
        pltpu.make_async_copy(source, target, load_sem.at[i])
        for i, (source, target) in enumerate((
            (grad_hbm, grad_ref), (mask_hbm, mask_ref), (index_hbm, index_ref),
            (feat_hbm, feats.at[c]), (weight_hbm, weight_ref), (tiles_hbm, tiles),
        ))
    ]
    for fetch in fetches:
        fetch.start()

    barrier = pltpu.get_barrier_semaphore()
    loop(1, N_COL, lambda d: pl.semaphore_signal(barrier, inc=1, device_id=(col(d), r), device_id_type=MESH))
    loop(1, N_ROW, lambda d: pl.semaphore_signal(barrier, inc=1, device_id=(c, row(d)), device_id_type=MESH))

    fetches[0].wait()
    fetches[1].wait()
    grad = grad_ref[...].astype(jnp.float32) * mask_ref[...].astype(jnp.float32)
    grad_t = jnp.transpose(grad).astype(jnp.bfloat16)
    for h in range(2):
        for e in range(2):
            stripe[h][2 * r + e] = grad_t[h * BLK:(h + 1) * BLK, e * BLK:(e + 1) * BLK]
        parts[h, SLOTS] = jnp.zeros((BLK, BLK), jnp.float32)
    fetches[2].wait()
    fetches[3].wait()

    pl.semaphore_wait(barrier, N_ROW - 1 + N_COL - 1)

    def peer(a, b):
        dx = a * (1 - k) + b * k
        dy = a * k + b * (1 - k)
        return (lax.rem(x + dx, 4) * 4 + lax.rem(y + dy, 4)) * 2 + k

    sibling = r + 1 - 2 * k

    def unit(h, at):
        return stripe[h].at[pl.ds(2 * at, 2)]

    def push(h, at, target, number):
        copy(unit(h, at), unit(h, at), g_send.at[h, number], g_recv.at[h, at], (c, target)).start()

    def arrived(h, at):
        copy(unit(h, at), unit(h, at), g_send.at[h, 0], g_recv.at[h, at], (c, sibling)).wait_recv()

    order = (1, 3, 2)

    def gather_start(h):
        for i, a in enumerate(order):
            push(h, r, peer(a, 0), i)
        for i, b in enumerate(order):
            push(h, r, peer(0, b), 3 + i)
        push(h, r, sibling, 6)

    def gather_first(h):
        for i, a in enumerate(order):
            at = peer(4 - a, 0)
            arrived(h, at)
            for j, b in enumerate(order):
                push(h, at, peer(0, b), 7 + 4 * i + j)
            push(h, at, sibling, 7 + 4 * i + 3)

    def gather_second(h, j):
        for i, a in enumerate((0,) + order):
            at = peer((4 - a) % 4, 4 - order[j])
            arrived(h, at)
            push(h, at, sibling, 19 + 4 * j + i)

    def gather_end(h):
        loop(0, N_ROW // 2, lambda i: arrived(h, 2 * i + 1 - k))

    def gather_sent(h):
        loop(0, 31, lambda i: copy(
            unit(h, r), unit(h, r), g_send.at[h, i], g_recv.at[h, r], (c, sibling)).wait_send())

    def feature(q, way, far):
        origin = col(-SIGN[way] * far)
        held = feats.at[origin, pl.ds(q * PIECE, PIECE)]
        return copy(held, held, f_send.at[q, way, far], f_recv.at[q, origin], (col(SIGN[way]), r))

    def feature_step(far):
        for q in range(PIECES):
            for way in range(2):
                if far < farthest(q, way):
                    if far > 0:
                        feature(q, way, far).wait_recv()
                    feature(q, way, far).start()

    def feature_end():
        for q in range(PIECES):
            for way in range(2):
                feature(q, way, farthest(q, way)).wait_recv()

    def feature_sent():
        for q in range(PIECES):
            for way in range(2):
                loop(0, farthest(q, way), lambda far: feature(q, way, far).wait_send())

    def positions():
        index = index_ref[...]
        down = lax.broadcasted_iota(jnp.int32, (SLOTS, SLOTS), 0)
        across = lax.broadcasted_iota(jnp.int32, (SLOTS, SLOTS), 1)
        column = jnp.broadcast_to(lax.rem(index, COLB), (SLOTS, SLOTS))
        column_down = jnp.sum(jnp.where(down == across, column, 0), axis=1, keepdims=True)
        column_down = jnp.broadcast_to(column_down, (SLOTS, SLOTS))
        previous = jnp.max(
            jnp.where((column == column_down) & (down < across), down, -1), axis=0, keepdims=True
        )
        last = jnp.max(
            jnp.where((column_down == across) & (down < count[0, 0]), down, -1), axis=0, keepdims=True
        )
        meta_v[...] = jnp.zeros_like(meta_v)
        meta_v[0:1, 0:SLOTS] = lax.div(index, COLB)
        meta_v[1:2, 0:SLOTS] = jnp.where(previous < 0, SLOTS, previous)
        meta_v[2:3, 0:SLOTS] = jnp.where(last < 0, SLOTS, last)
        pltpu.make_async_copy(meta_v, meta, meta_sem).start()

    def products(h, begin=0, end=SLOTS):
        def some(i):
            for j in range(GROUP):
                n = i * GROUP + j
                got = jnp.dot(stripe[h][meta[0, n]], tiles[n], preferred_element_type=jnp.float32)
                parts[h, n] = got + parts[h, meta[1, n]]
        loop(begin // GROUP, end // GROUP, some)

    def own(h, s, e):
        return parts[h, meta[2, 2 * s + e]]

    def message(h, e, way, far):
        slot = (h, e, way, far - 1)
        return copy(
            sums_out.at[slot], sums_in.at[slot], s_send.at[slot], s_recv.at[slot], (col(SIGN[way]), r)
        )

    def received(h, e, way, far):
        message(h, e, way, far).wait_recv()
        return sums_in[h, e, way, far - 1].astype(jnp.float32)

    def chain(h, far):
        for e in range(2):
            for way in range(2):
                most = farthest(e, way)
                if far <= most:
                    value = own(h, col(SIGN[way] * far), e)
                    if far < most:
                        value = value + received(h, e, way, far + 1)
                    sums_out[h, e, way, far - 1] = value.astype(jnp.bfloat16)
                    message(h, e, way, far).start()

    def finish(h):
        for e in range(2):
            value = own(h, c, e)
            for way in range(2):
                value = value + received(h, e, way, 1)
            node_t[h * BLK:(h + 1) * BLK, e * BLK:(e + 1) * BLK] = value

    def sums_sent(h):
        for e in range(2):
            for way in range(2):
                loop(1, farthest(e, way) + 1, lambda far: message(h, e, way, far).wait_send())

    def weight_term(begin, end):
        if begin == 0:
            total[...] = jnp.zeros_like(total)

        def one(s):
            terms = jnp.concatenate([
                jnp.concatenate([own(h, s, e).astype(jnp.bfloat16) for e in range(2)], axis=1)
                for h in range(2)
            ], axis=0)
            total[...] += jnp.dot(terms, feats[s], preferred_element_type=jnp.float32)

        loop(begin, end, one)
        if end == N_COL:
            dw[...] = total[...].reshape(N_ROW, F // N_ROW, F)

    def term(at):
        return copy(dw.at[at], plane_in.at[r], a_send.at[at], a_recv.at[r], (c, at))

    def term_from(at):
        return copy(dw.at[at], plane_in.at[at], a_send.at[at], a_recv.at[at], (c, at))

    def along(at):
        return copy(line.at[c], line.at[c], z_send.at[at], z_recv.at[c], (at, r))

    def along_from(at):
        return copy(line.at[at], line.at[at], z_send.at[at], z_recv.at[at], (at, r))

    def back(at):
        return copy(done.at[r], done.at[r], b_send.at[at], b_recv.at[r], (c, at))

    def back_from(at):
        return copy(done.at[at], done.at[at], b_send.at[at], b_recv.at[at], (c, at))

    def share_plane():
        loop(1, N_ROW, lambda d: term(row(d)).start())
        plane_in[r] = dw[r]

    def share_line():
        loop(1, N_ROW, lambda d: term_from(row(d)).wait_recv())
        mine = jnp.sum(plane_in[...], axis=0)
        mine = jnp.concatenate([mine[:, :BLK], mine[:, BLK:]], axis=0)
        line[c] = mine.astype(jnp.bfloat16)
        loop(1, N_COL, lambda d: along(col(d)).start())

    def share_back():
        loop(1, N_COL, lambda d: along_from(col(d)).wait_recv())
        whole = jnp.sum(line[...].astype(jnp.float32), axis=0)
        done[r] = jnp.concatenate([whole[:F // N_ROW], whole[F // N_ROW:]], axis=1)
        loop(1, N_ROW, lambda d: back(row(d)).start())

    gather_start(0)
    feature_step(0)
    gather_start(1)
    positions()
    gather_first(0)
    feature_step(1)
    gather_first(1)
    feature_step(2)
    gather_second(0, 0)
    feature_step(3)
    gather_second(0, 1)
    gather_second(0, 2)
    feature_step(4)
    gather_second(1, 0)
    gather_second(1, 1)
    feature_step(5)
    gather_second(1, 2)
    fetches[4].wait()
    fetches[5].wait()
    pltpu.make_async_copy(meta_v, meta, meta_sem).wait()
    gather_end(0)
    feature_step(6)
    products(0, 0, SLOTS // 2)
    feature_step(7)
    products(0, SLOTS // 2, SLOTS)
    chain(0, 8)
    gather_end(1)
    products(1, 0, SLOTS // 2)
    chain(0, 7)
    products(1, SLOTS // 2, SLOTS)
    chain(1, 8)
    chain(0, 6)
    feature_end()
    weight_term(0, N_COL // 2)
    chain(1, 7)
    chain(0, 5)
    weight_term(N_COL // 2, N_COL)
    share_plane()
    chain(1, 6)
    chain(0, 4)
    gather_sent(0)
    gather_sent(1)
    chain(1, 5)
    chain(0, 3)
    share_line()
    chain(1, 4)
    chain(0, 2)
    feature_sent()
    chain(1, 3)
    chain(0, 1)
    chain(1, 2)
    finish(0)
    chain(1, 1)
    sums_sent(0)
    share_back()
    finish(1)
    node = jnp.transpose(node_t[...])
    high = node.astype(jnp.bfloat16)
    low = (node - high.astype(jnp.float32)).astype(jnp.bfloat16)
    input_out[...] = sum(
        lax.dot_general(half, weight_ref[...], (((1,), (1,)), ((), ())), preferred_element_type=jnp.float32)
        for half in (high, low)
    ).astype(jnp.bfloat16)
    sums_sent(1)
    loop(1, N_ROW, lambda d: term(row(d)).wait_send())
    loop(1, N_COL, lambda d: along(col(d)).wait_send())
    loop(1, N_ROW, lambda d: back_from(row(d)).wait_recv())
    weight_out[...] = done[...].reshape(F, F)
    loop(1, N_ROW, lambda d: back(row(d)).wait_send())


def on_device(out_grad, relu_mask, features, weight, tile_values, tile_index, tile_count):
    vmem = pl.BlockSpec(memory_space=pltpu.VMEM)
    anywhere = pl.BlockSpec(memory_space=pl.ANY)
    dma = pltpu.SemaphoreType.DMA
    bf16, f32, i32 = jnp.bfloat16, jnp.float32, jnp.int32
    input_grad, weight_t = pl.pallas_call(
        kernel,
        name="layer_backward",
        out_shape=(jax.ShapeDtypeStruct((F, F), bf16), jax.ShapeDtypeStruct((F, F), f32)),
        in_specs=[pl.BlockSpec(memory_space=pltpu.SMEM)] + [anywhere] * 6,
        out_specs=(vmem, vmem),
        scratch_shapes=[
            pltpu.VMEM((1, SLOTS), i32),
            pltpu.VMEM((8, BLK), i32),
            pltpu.SMEM((8, BLK), i32),
            pltpu.VMEM((F, F), bf16),
            pltpu.VMEM((F, F), i32),
            pltpu.VMEM((N_COL, F, F), bf16),
            pltpu.VMEM((F, F), bf16),
            pltpu.VMEM((SLOTS, BLK, BLK), bf16),
            pltpu.VMEM((STRIPE, BLK, BLK), bf16),
            pltpu.VMEM((STRIPE, BLK, BLK), bf16),
            pltpu.VMEM((2, SLOTS + 1, BLK, BLK), f32),
            pltpu.VMEM((2, 2, 2, HALF, BLK, BLK), bf16),
            pltpu.VMEM((2, 2, 2, HALF, BLK, BLK), bf16),
            pltpu.VMEM((F, F), f32),
            pltpu.VMEM((F, F), f32),
            pltpu.VMEM((N_ROW, F // N_ROW, F), f32),
            pltpu.VMEM((N_ROW, F // N_ROW, F), f32),
            pltpu.VMEM((N_COL, 2 * F // N_ROW, BLK), bf16),
            pltpu.VMEM((N_ROW, F // N_ROW, F), f32),
            dma((6,)), dma, dma((2, 31)), dma((2, N_ROW)), dma((PIECES, 2, HALF)), dma((PIECES, N_COL)),
            dma((2, 2, 2, HALF)), dma((2, 2, 2, HALF)),
            dma((N_ROW,)), dma((N_ROW,)), dma((N_COL,)), dma((N_COL,)), dma((N_ROW,)), dma((N_ROW,)),
        ],
        compiler_params=pltpu.CompilerParams(
            collective_id=0, has_side_effects=True, vmem_limit_bytes=60 * 2**20
        ),
        cost_estimate=pl.CostEstimate(flops=2 * 10**9, bytes_accessed=8 * 2**20, transcendentals=0),
    )(
        tile_count, tile_index.reshape(1, SLOTS), out_grad, relu_mask, features, weight,
        tile_values.reshape(SLOTS, BLK, BLK),
    )
    return input_grad, weight_t.T


def solution(mesh):
    placed = (
        P(("col", "row"), None),
        P(("col", "row"), None),
        P(("col", "row"), None),
        P(),
        P("col", "row", None, None, None),
        P("col", "row", None),
        P("col", "row"),
    )
    return jax.shard_map(
        on_device,
        mesh=mesh,
        in_specs=placed,
        out_specs=(P(("col", "row"), None), P()),
        check_vma=False,
    )
```

time: 687 us -> 97.9 us (0.14)
  waiting for transfers between devices: 603 us -> 0 us
  Pallas kernels: 0 us -> 93.1 us
  other arithmetic: 30.7 us -> 0 us
  local copies, waits for them, and re-layouts: 25 us -> 3.35 us
  between operations: 14.4 us -> 1.29 us
  matrix products: 12.8 us -> 0 us
    psum x1 -> x0, waiting for transfers between devices: 466 us -> none  [on_device(): weight_grad = lax.psum(local_weight, ('col', 'row'))]
    pallas_call x0 -> x1, Pallas kernels: none -> 93.1 us  [on_device(): pl.pallas_call(kernel, name='layer_backward', out_shape=(jax.ShapeDtypeSt...]
    reduce_scatter x1 -> x0, waiting for transfers between devices: 68.4 us -> none  [on_device(): lax.psum_scatter(partial_value, 'col', scatter_dimension=0, tiled=True)]
    all_gather x1 -> x0, waiting for transfers between devices: 68.4 us -> none  [on_device(): stripe = lax.all_gather(gradient, 'row', axis=0, tiled=True)]
    scatter-add x1 -> x0, other arithmetic: 28.3 us -> none  [on_device(): partial_value = jnp.zeros((col_blocks, block_size, width), jnp.float32).a...]
    dot_general x3 -> x0, matrix products: 12.8 us -> none  [the longest x1 9.09 us: on_device(): jnp.einsum('kab,kaf->kbf', tile_block, stripe_blocks[row_block], preferre...]
    dot_general x1 -> x0, local copies, waits for them, and re-layouts: 12.6 us -> none  [on_device(): jnp.einsum('kab,kaf->kbf', tile_block, stripe_blocks[row_block], preferre...]
    gather x1 -> x0, local copies, waits for them, and re-layouts: 8.18 us -> none  [on_device(): stripe_blocks[row_block]]
  transfers between devices with their start and end apart: 3 -> 0, of which waited for: 3 -> 0; matrix products, arithmetic and copies ran while one was open for 0% -> 0% of each run, Pallas kernels for 0% -> 0%
where the time goes in v1:
time: 97.9 us; the launch traced here: 97.7 us
  Pallas kernels  93.1 us (95%)
  local copies, waits for them, and re-layouts  3.35 us (3%)
  between operations  1.29 us (1%)
    pallas_call x1, Pallas kernels, on_device(): pl.pallas_call(kernel, name='layer_backward', out_shape=(jax.ShapeDtypeSt...  93.1 us
    unnamed x2, local copies, waits for them, and re-layouts  3.35 us

profile of v1, /device:TPU:1, one launch (start us, length us, event | category | flops | bytes accessed | tf_op | source)
XLA Modules:
  0.0 97.7 jit_solution(18128208259393269997)
XLA Ops:
  1.3 93.1 %layer_backward.1 = (bf16[256,256]{1,0:T(8,128)(2,1)}, f32[256,256]{1,0:T(8,128)}) custom-call(s32[1,1]{1,0:T(1,128)S(6)} %copy.11.count, s32[1,96]{1,0:T(1,128)} %bitcast.5, bf16[256,256]{1,0:T(8,128)(2,1)} %grad_hbm.1, s32[256,256]{1,0:T(8,128)} %mask_hbm.1, bf16[256,256]{1,0:T(8,128)(2,1)} %feat_hbm.1, bf16[256,256]{1,0:T(8,128)(2,1)} %weight_hbm.1, ...), custom_call_target="tpu_custom_call" | custom-call | flops 2000000000 | bytes 8388608 | tf_op jit(solution)/shard_map/layer_backward/pallas_call | solution.py:344
  94.3 1.8 %copy.9 = f32[256,256]{1,0:T(8,128)} copy(f32[256,256]{0,1:T(8,128)} %bitcast.3) | data formatting | bytes 524288
  96.1 1.6 %copy.12 = bf16[256,256]{1,0:T(8,128)(2,1)} copy(bf16[256,256]{1,0:T(8,128)(2,1)} %get-tuple-element.10) | data formatting | bytes 262144

commit v2 on v1

--- a/solution.py
+++ b/solution.py
@@ -14,9 +14,10 @@
 COLB = 32
 STRIPE = 64
 HALF = N_COL // 2
-GROUP = 4
+GROUP = 8
 PIECES = 4
 PIECE = F // PIECES
+RADIUS = 7
 SIGN = (1, -1)
 
 
@@ -137,20 +138,19 @@
     def feature_step(far):
         for q in range(PIECES):
             for way in range(2):
-                if far < farthest(q, way):
-                    if far > 0:
-                        feature(q, way, far).wait_recv()
-                    feature(q, way, far).start()
+                if far > 0:
+                    feature(q, way, far).wait_recv()
+                feature(q, way, far).start()
 
     def feature_end():
         for q in range(PIECES):
             for way in range(2):
-                feature(q, way, farthest(q, way)).wait_recv()
+                feature(q, way, RADIUS).wait_recv()
 
     def feature_sent():
         for q in range(PIECES):
             for way in range(2):
-                loop(0, farthest(q, way), lambda far: feature(q, way, far).wait_send())
+                loop(0, RADIUS, lambda far: feature(q, way, far).wait_send())
 
     def positions():
         index = index_ref[...]
@@ -215,20 +215,29 @@
             for way in range(2):
                 loop(1, farthest(e, way) + 1, lambda far: message(h, e, way, far).wait_send())
 
-    def weight_term(begin, end):
-        if begin == 0:
-            total[...] = jnp.zeros_like(total)
-
-        def one(s):
-            terms = jnp.concatenate([
-                jnp.concatenate([own(h, s, e).astype(jnp.bfloat16) for e in range(2)], axis=1)
-                for h in range(2)
-            ], axis=0)
-            total[...] += jnp.dot(terms, feats[s], preferred_element_type=jnp.float32)
-
-        loop(begin, end, one)
-        if end == N_COL:
-            dw[...] = total[...].reshape(N_ROW, F // N_ROW, F)
+    def joined(part):
+        return jnp.concatenate([
+            jnp.concatenate([part(h, e).astype(jnp.bfloat16) for e in range(2)], axis=1) for h in range(2)
+        ], axis=0)
+
+    def weight_near():
+        def at(s):
+            terms = joined(lambda h, e: own(h, s, e))
+            return jnp.dot(terms, feats[s], preferred_element_type=jnp.float32)
+
+        total[...] = at(c)
+
+        def both(j):
+            total[...] += at(col(j)) + at(col(-j))
+
+        loop(1, RADIUS, both)
+
+    def weight_far():
+        got = total[...]
+        for way in range(2):
+            terms = joined(lambda h, e: sums_out[h, e, way, RADIUS - 1])
+            got = got + jnp.dot(terms, feats[col(SIGN[way] * RADIUS)], preferred_element_type=jnp.float32)
+        dw[...] = got.reshape(N_ROW, F // N_ROW, F)
 
     def term(at):
         return copy(dw.at[at], plane_in.at[r], a_send.at[at], a_recv.at[r], (c, at))
@@ -267,59 +276,58 @@
 
     gather_start(0)
     feature_step(0)
+    positions()
+    feature_step(1)
+    gather_first(0)
     gather_start(1)
-    positions()
-    gather_first(0)
-    feature_step(1)
-    gather_first(1)
     feature_step(2)
     gather_second(0, 0)
     feature_step(3)
+    gather_first(1)
     gather_second(0, 1)
     gather_second(0, 2)
     feature_step(4)
-    gather_second(1, 0)
-    gather_second(1, 1)
-    feature_step(5)
-    gather_second(1, 2)
     fetches[4].wait()
     fetches[5].wait()
     pltpu.make_async_copy(meta_v, meta, meta_sem).wait()
     gather_end(0)
-    feature_step(6)
     products(0, 0, SLOTS // 2)
-    feature_step(7)
+    feature_step(5)
+    gather_second(1, 0)
+    gather_second(1, 1)
     products(0, SLOTS // 2, SLOTS)
     chain(0, 8)
+    feature_step(6)
+    gather_second(1, 2)
     gather_end(1)
     products(1, 0, SLOTS // 2)
     chain(0, 7)
     products(1, SLOTS // 2, SLOTS)
     chain(1, 8)
+    feature_end()
+    weight_near()
     chain(0, 6)
-    feature_end()
-    weight_term(0, N_COL // 2)
     chain(1, 7)
+    weight_far()
+    share_plane()
     chain(0, 5)
-    weight_term(N_COL // 2, N_COL)
-    share_plane()
     chain(1, 6)
+    gather_sent(0)
     chain(0, 4)
-    gather_sent(0)
+    chain(1, 5)
+    share_line()
     gather_sent(1)
-    chain(1, 5)
     chain(0, 3)
-    share_line()
     chain(1, 4)
+    feature_sent()
     chain(0, 2)
-    feature_sent()
     chain(1, 3)
     chain(0, 1)
     chain(1, 2)
+    share_back()
     finish(0)
     chain(1, 1)
     sums_sent(0)
-    share_back()
     finish(1)
     node = jnp.transpose(node_t[...])
     high = node.astype(jnp.bfloat16)
@@ -367,7 +375,7 @@
             pltpu.VMEM((N_ROW, F // N_ROW, F), f32),
             pltpu.VMEM((N_COL, 2 * F // N_ROW, BLK), bf16),
             pltpu.VMEM((N_ROW, F // N_ROW, F), f32),
-            dma((6,)), dma, dma((2, 31)), dma((2, N_ROW)), dma((PIECES, 2, HALF)), dma((PIECES, N_COL)),
+            dma((6,)), dma, dma((2, 31)), dma((2, N_ROW)), dma((PIECES, 2, RADIUS)), dma((PIECES, N_COL)),
             dma((2, 2, 2, HALF)), dma((2, 2, 2, HALF)),
             dma((N_ROW,)), dma((N_ROW,)), dma((N_COL,)), dma((N_COL,)), dma((N_ROW,)), dma((N_ROW,)),
         ],

time: 97.9 us -> 86.2 us (0.88)
  Pallas kernels: 93.1 us -> 81.4 us
    pallas_call x1, Pallas kernels: 93.1 us -> 81.4 us  [on_device(): pl.pallas_call(kernel, name='layer_backward', out_shape=(jax.ShapeDtypeSt...]
where the time goes in v2:
time: 86.2 us; the launch traced here: 86 us
  Pallas kernels  81.4 us (94%)
  local copies, waits for them, and re-layouts  3.35 us (4%)
  between operations  1.29 us (1%)
    pallas_call x1, Pallas kernels, on_device(): pl.pallas_call(kernel, name='layer_backward', out_shape=(jax.ShapeDtypeSt...  81.4 us
    unnamed x2, local copies, waits for them, and re-layouts  3.35 us

profile of v2, /device:TPU:1, one launch (start us, length us, event | category | flops | bytes accessed | tf_op | source)
XLA Modules:
  0.0 86.0 jit_solution(10775582780265916697)
XLA Ops:
  1.3 81.4 %layer_backward.1 = (bf16[256,256]{1,0:T(8,128)(2,1)}, f32[256,256]{1,0:T(8,128)}) custom-call(s32[1,1]{1,0:T(1,128)S(6)} %copy.11.count, s32[1,96]{1,0:T(1,128)} %bitcast.5, bf16[256,256]{1,0:T(8,128)(2,1)} %grad_hbm.1, s32[256,256]{1,0:T(8,128)} %mask_hbm.1, bf16[256,256]{1,0:T(8,128)(2,1)} %feat_hbm.1, bf16[256,256]{1,0:T(8,128)(2,1)} %weight_hbm.1, ...), custom_call_target="tpu_custom_call" | custom-call | flops 2000000000 | bytes 8388608 | tf_op jit(solution)/shard_map/layer_backward/pallas_call | solution.py:352
  82.7 1.8 %copy.9 = f32[256,256]{1,0:T(8,128)} copy(f32[256,256]{0,1:T(8,128)} %bitcast.3) | data formatting | bytes 524288
  84.5 1.6 %copy.12 = bf16[256,256]{1,0:T(8,128)(2,1)} copy(bf16[256,256]{1,0:T(8,128)(2,1)} %get-tuple-element.10) | data formatting | bytes 262144

commit v3 on v2

--- a/solution.py
+++ b/solution.py
@@ -14,10 +14,11 @@
 COLB = 32
 STRIPE = 64
 HALF = N_COL // 2
-GROUP = 8
+GROUP = 16
 PIECES = 4
 PIECE = F // PIECES
 RADIUS = 7
+JOINS = (2,)
 SIGN = (1, -1)
 
 
@@ -182,11 +183,17 @@
     def own(h, s, e):
         return parts[h, meta[2, 2 * s + e]]
 
+    def skips(h, far):
+        return h == 1 and far in JOINS
+
     def message(h, e, way, far):
         slot = (h, e, way, far - 1)
         return copy(
-            sums_out.at[slot], sums_in.at[slot], s_send.at[slot], s_recv.at[slot], (col(SIGN[way]), r)
+            sums_out.at[slot], sums_in.at[slot], s_send.at[slot], s_recv.at[slot], (col(SIGN[way] * (2 if skips(h, far) else 1)), r)
         )
+
+    def arrives(h, before, far):
+        return before - far == (2 if skips(h, before) else 1)
 
     def received(h, e, way, far):
         message(h, e, way, far).wait_recv()
@@ -198,8 +205,9 @@
                 most = farthest(e, way)
                 if far <= most:
                     value = own(h, col(SIGN[way] * far), e)
-                    if far < most:
-                        value = value + received(h, e, way, far + 1)
+                    for before in (far + 1, far + 2):
+                        if before <= most and arrives(h, before, far):
+                            value = value + received(h, e, way, before)
                     sums_out[h, e, way, far - 1] = value.astype(jnp.bfloat16)
                     message(h, e, way, far).start()
 
@@ -207,13 +215,16 @@
         for e in range(2):
             value = own(h, c, e)
             for way in range(2):
-                value = value + received(h, e, way, 1)
+                for before in (1, 2):
+                    if arrives(h, before, 0):
+                        value = value + received(h, e, way, before)
             node_t[h * BLK:(h + 1) * BLK, e * BLK:(e + 1) * BLK] = value
 
     def sums_sent(h):
         for e in range(2):
             for way in range(2):
-                loop(1, farthest(e, way) + 1, lambda far: message(h, e, way, far).wait_send())
+                for far in range(1, farthest(e, way) + 1):
+                    message(h, e, way, far).wait_send()
 
     def joined(part):
         return jnp.concatenate([
@@ -237,7 +248,8 @@
         for way in range(2):
             terms = joined(lambda h, e: sums_out[h, e, way, RADIUS - 1])
             got = got + jnp.dot(terms, feats[col(SIGN[way] * RADIUS)], preferred_element_type=jnp.float32)
-        dw[...] = got.reshape(N_ROW, F // N_ROW, F)
+        got = got.reshape(N_ROW, F // N_ROW, F)
+        dw[...] = jnp.concatenate([got[:, :, :BLK], got[:, :, BLK:]], axis=1).astype(jnp.bfloat16)
 
     def term(at):
         return copy(dw.at[at], plane_in.at[r], a_send.at[at], a_recv.at[r], (c, at))
@@ -263,15 +275,12 @@
 
     def share_line():
         loop(1, N_ROW, lambda d: term_from(row(d)).wait_recv())
-        mine = jnp.sum(plane_in[...], axis=0)
-        mine = jnp.concatenate([mine[:, :BLK], mine[:, BLK:]], axis=0)
-        line[c] = mine.astype(jnp.bfloat16)
+        line[c] = jnp.sum(plane_in[...].astype(jnp.float32), axis=0).astype(jnp.bfloat16)
         loop(1, N_COL, lambda d: along(col(d)).start())
 
     def share_back():
         loop(1, N_COL, lambda d: along_from(col(d)).wait_recv())
-        whole = jnp.sum(line[...].astype(jnp.float32), axis=0)
-        done[r] = jnp.concatenate([whole[:F // N_ROW], whole[F // N_ROW:]], axis=1)
+        done[r] = jnp.sum(line[...].astype(jnp.float32), axis=0).astype(jnp.bfloat16)
         loop(1, N_ROW, lambda d: back(row(d)).start())
 
     gather_start(0)
@@ -322,11 +331,11 @@
     feature_sent()
     chain(0, 2)
     chain(1, 3)
+    chain(1, 1)
     chain(0, 1)
+    share_back()
     chain(1, 2)
-    share_back()
     finish(0)
-    chain(1, 1)
     sums_sent(0)
     finish(1)
     node = jnp.transpose(node_t[...])
@@ -340,8 +349,16 @@
     loop(1, N_ROW, lambda d: term(row(d)).wait_send())
     loop(1, N_COL, lambda d: along(col(d)).wait_send())
     loop(1, N_ROW, lambda d: back_from(row(d)).wait_recv())
-    weight_out[...] = done[...].reshape(F, F)
+    whole = done[...].astype(jnp.float32)
+    weight_out[...] = jnp.concatenate(
+        [whole[:, :F // N_ROW], whole[:, F // N_ROW:]], axis=2
+    ).reshape(F, F)
     loop(1, N_ROW, lambda d: back(row(d)).wait_send())
+
+
+def place(input_ref, weight_ref, input_out, weight_out):
+    input_out[...] = input_ref[...]
+    weight_out[...] = jnp.transpose(weight_ref[...])
 
 
 def on_device(out_grad, relu_mask, features, weight, tile_values, tile_index, tile_count):
@@ -371,10 +388,10 @@
             pltpu.VMEM((2, 2, 2, HALF, BLK, BLK), bf16),
             pltpu.VMEM((F, F), f32),
             pltpu.VMEM((F, F), f32),
-            pltpu.VMEM((N_ROW, F // N_ROW, F), f32),
-            pltpu.VMEM((N_ROW, F // N_ROW, F), f32),
+            pltpu.VMEM((N_ROW, 2 * F // N_ROW, BLK), bf16),
+            pltpu.VMEM((N_ROW, 2 * F // N_ROW, BLK), bf16),
             pltpu.VMEM((N_COL, 2 * F // N_ROW, BLK), bf16),
-            pltpu.VMEM((N_ROW, F // N_ROW, F), f32),
+            pltpu.VMEM((N_ROW, 2 * F // N_ROW, BLK), bf16),
             dma((6,)), dma, dma((2, 31)), dma((2, N_ROW)), dma((PIECES, 2, RADIUS)), dma((PIECES, N_COL)),
             dma((2, 2, 2, HALF)), dma((2, 2, 2, HALF)),
             dma((N_ROW,)), dma((N_ROW,)), dma((N_COL,)), dma((N_COL,)), dma((N_ROW,)), dma((N_ROW,)),
@@ -387,7 +404,13 @@
         tile_count, tile_index.reshape(1, SLOTS), out_grad, relu_mask, features, weight,
         tile_values.reshape(SLOTS, BLK, BLK),
     )
-    return input_grad, weight_t.T
+    return pl.pallas_call(
+        place,
+        name="place",
+        out_shape=(jax.ShapeDtypeStruct((F, F), bf16), jax.ShapeDtypeStruct((F, F), f32)),
+        in_specs=[vmem, vmem],
+        out_specs=(vmem, vmem),
+    )(input_grad, weight_t)
 
 
 def solution(mesh):

time: 86.2 us -> 82.2 us (0.954)
  local copies, waits for them, and re-layouts: 3.35 us -> 0 us
    unnamed x2 -> x0, local copies, waits for them, and re-layouts: 3.35 us -> none
    pallas_call x1, Pallas kernels: 81.4 us -> 78.9 us  [on_device(): pl.pallas_call(kernel, name='layer_backward', out_shape=(jax.ShapeDtypeSt...]
    pallas_call x0 -> x1, Pallas kernels: none -> 1.86 us  [on_device(): pl.pallas_call(place, name='place', out_shape=(jax.ShapeDtypeStruct((F, F...]
where the time goes in v3:
time: 82.2 us; the launch traced here: 82 us
  Pallas kernels  80.7 us (98%)
  between operations  1.29 us (2%)
    pallas_call x1, Pallas kernels, on_device(): pl.pallas_call(kernel, name='layer_backward', out_shape=(jax.ShapeDtypeSt...  78.9 us
    pallas_call x1, Pallas kernels, on_device(): pl.pallas_call(place, name='place', out_shape=(jax.ShapeDtypeStruct((F, F...  1.86 us

profile of v3, /device:TPU:1, one launch (start us, length us, event | category | flops | bytes accessed | tf_op | source)
XLA Modules:
  0.0 82.0 jit_solution(4439993948847893138)
XLA Ops:
  1.3 78.9 %layer_backward.1 = (bf16[256,256]{1,0:T(8,128)(2,1)}, f32[256,256]{1,0:T(8,128)}) custom-call(s32[1,1]{1,0:T(1,128)S(6)} %copy.9.count, s32[1,96]{1,0:T(1,128)} %bitcast.3, bf16[256,256]{1,0:T(8,128)(2,1)} %grad_hbm.1, s32[256,256]{1,0:T(8,128)} %mask_hbm.1, bf16[256,256]{1,0:T(8,128)(2,1)} %feat_hbm.1, bf16[256,256]{1,0:T(8,128)(2,1)} %weight_hbm.1, ...), custom_call_target="tpu_custom_call" | custom-call | flops 2000000000 | bytes 8388608 | tf_op jit(solution)/shard_map/layer_backward/pallas_call | solution.py:369
  80.2 1.9 %place.1 = (bf16[256,256]{1,0:T(8,128)(2,1)}, f32[256,256]{1,0:T(8,128)}) custom-call(bf16[256,256]{1,0:T(8,128)(2,1)} %get-tuple-element.4.input_ref, f32[256,256]{1,0:T(8,128)} %get-tuple-element.5.weight_ref), custom_call_target="tpu_custom_call" | custom-call | tf_op jit(solution)/shard_map/place/pallas_call | solution.py:407

commit v4 on v3

--- a/solution.py
+++ b/solution.py
@@ -15,7 +15,7 @@
 STRIPE = 64
 HALF = N_COL // 2
 GROUP = 16
-PIECES = 4
+PIECES = 2
 PIECE = F // PIECES
 RADIUS = 7
 JOINS = (2,)

time: 82.2 us -> 82.4 us (level)
  no operation moved by 1% of the time
where the time goes in v4:
time: 82.4 us; the launch traced here: 82.1 us
  Pallas kernels  80.8 us (98%)
  between operations  1.29 us (2%)
    pallas_call x1, Pallas kernels, on_device(): pl.pallas_call(kernel, name='layer_backward', out_shape=(jax.ShapeDtypeSt...  78.9 us
    pallas_call x1, Pallas kernels, on_device(): pl.pallas_call(place, name='place', out_shape=(jax.ShapeDtypeStruct((F, F...  1.86 us

profile of v4, /device:TPU:1, one launch (start us, length us, event | category | flops | bytes accessed | tf_op | source)
XLA Modules:
  0.0 82.1 jit_solution(3585770952421578746)
XLA Ops:
  1.3 78.9 %layer_backward.1 = (bf16[256,256]{1,0:T(8,128)(2,1)}, f32[256,256]{1,0:T(8,128)}) custom-call(s32[1,1]{1,0:T(1,128)S(6)} %copy.9.count, s32[1,96]{1,0:T(1,128)} %bitcast.3, bf16[256,256]{1,0:T(8,128)(2,1)} %grad_hbm.1, s32[256,256]{1,0:T(8,128)} %mask_hbm.1, bf16[256,256]{1,0:T(8,128)(2,1)} %feat_hbm.1, bf16[256,256]{1,0:T(8,128)(2,1)} %weight_hbm.1, ...), custom_call_target="tpu_custom_call" | custom-call | flops 2000000000 | bytes 8388608 | tf_op jit(solution)/shard_map/layer_backward/pallas_call | solution.py:369
  80.2 1.9 %place.1 = (bf16[256,256]{1,0:T(8,128)(2,1)}, f32[256,256]{1,0:T(8,128)}) custom-call(bf16[256,256]{1,0:T(8,128)(2,1)} %get-tuple-element.4.input_ref, f32[256,256]{1,0:T(8,128)} %get-tuple-element.5.weight_ref), custom_call_target="tpu_custom_call" | custom-call | tf_op jit(solution)/shard_map/place/pallas_call | solution.py:407
